TPU v7x, 32 devices: a whole 2x2x4 slice. The times are simulated.
32 devices in a mesh: groups: 2 (over x), slab: 16 (over z, y, core).
Axes of the slice: x: 2, y: 2, z: 4, core: 2. Of those that a mesh axis runs over, the one named last changes fastest.
Arguments:
- slowness: float32 [64, 64, 128], P('slab', 'groups'), parts along dimension 1, may hold values from 0.5 to 2
- absorbing: int32 [64, 64, 128], P('slab', 'groups'), parts along dimension 1, may hold values 0 or 1
- src_cell: int32 [16], P('groups'), parts along dimension 0, may hold values from 0 to 262143
- src_amp: float32 [2, 16], P(None, 'groups'), parts along dimension 1, may hold values from -8 to 8
- rec_slab: int32 [16, 8192, 1], P('groups', 'slab'), parts along dimension 0, may hold values from 0 to 15; in each aligned block of 512 rows (0 to 511, 512 to 1023, ..., all dimensions but the last counted through in order) at most 96 rows name the same one
- rec_local: int32 [16, 8192], P('groups', 'slab'), parts along dimension 0, may hold values from 0 to 16383
- rec_data: float32 [2, 16, 8192], P(None, 'groups', 'slab'), parts along dimension 1, may hold values from -6 to 6
Outputs:
- wavefield: float32 [2, 16, 64, 32, 128], P(None, 'groups', 'slab'), parts along dimension 1
- updated: float32 [64, 64, 128], P('slab', 'groups'), parts along dimension 1
There are 2 independent parts, one for each index of `groups`. A program takes and returns all parts, laid end to end along the dimension named above; each array names one. Nothing has to cross between parts.
Inputs may be any that keep to these rules, and one draw needn't show every extreme that they name: `rec_slab`: for each shot, among the 512 receivers of one aligned block of the receiver list, at most 96 lie in one slab; some block holds exactly 96 in some slab.
All inputs are finite; a program needn't handle non-finite values. No bound on the sum of `absorbing` on one device may be relied on, other than what follows from the above.
Results may differ from a plain program's by a relative error of at most 0.0001.
Values sent between devices are 32-bit elements; how exact they have to be, the bound alone decides.
A program may use at most 192 MiB of HBM per device.

v0:
```python
import jax
import jax.numpy as jnp
from jax import lax
from jax.sharding import PartitionSpec as P

ITERS = 2


K_SQ = 0.8
DAMPING = 0.6
PENALTY = 4.0
REGULAR = 0.5


def padded_2(block, sides, width):
    for axis, dim in sides:
        count = lax.axis_size(axis)
        forward = [(i, i + 1) for i in range(count - 1)]
        backward = [(target, source) for source, target in forward]
        low = lax.ppermute(
            lax.slice_in_dim(block, block.shape[dim] - width, None, axis=dim), axis, forward
        )
        high = lax.ppermute(lax.slice_in_dim(block, 0, width, axis=dim), axis, backward)
        block = jnp.concatenate([low, block, high], axis=dim)
    return block


def laplace(extended):
    center = extended[:, :, 1:-1]
    padded = jnp.pad(center, ((0, 0), (0, 0), (0, 0), (1, 1), (1, 1)))
    beside = extended[:, :, 2:] + extended[:, :, :-2]
    beside = beside + padded[:, :, :, 2:, 1:-1] + padded[:, :, :, :-2, 1:-1]
    beside = beside + padded[:, :, :, 1:-1, 2:] + padded[:, :, :, 1:-1, :-2]
    return (6.0 * center - beside, center)


def helmholtz(extended, coeff, lossy, sign):
    lap, center = laplace(extended)
    real_part = lap[0] - coeff * center[0] + sign * lossy * center[1]
    imag_part = lap[1] - coeff * center[1] - sign * lossy * center[0]
    return jnp.stack([real_part, imag_part])


def inner(left, right):
    return jnp.sum(left * right, axis=(0, 2, 3, 4))


def squares(residual):
    return lax.psum(inner(residual, residual), "slab")


def expand(values):
    return values[None, :, None, None, None]


def local(slowness, absorbing, src_cell, src_amp, rec_slab, rec_local, rec_data):
    count = lax.axis_size("slab")
    index = lax.axis_index("slab")
    depth, height, width = slowness.shape
    cells = depth * height * width
    shots = src_amp.shape[1]
    mask_f = absorbing.astype(jnp.float32)
    coeff = K_SQ * slowness
    lossy = DAMPING * coeff * mask_f
    owner = rec_slab[:, :, 0]
    block = rec_local.shape[1]
    capacity = 3 * block // count
    packed = jnp.stack(
        [owner.astype(jnp.float32), rec_local.astype(jnp.float32), rec_data[0], rec_data[1]]
    )
    table = lax.all_gather(packed, "slab", axis=2, tiled=True)
    grouped = table.reshape(4, shots, count, block)
    mine = (grouped[0].astype(jnp.int32) == index).astype(jnp.int32)
    order = jnp.arange(block, dtype=jnp.int32)
    score = mine * block + (block - 1 - order)[None, None, :]
    unused, picks = lax.top_k(score, capacity)
    chosen = jnp.take_along_axis(
        grouped, jnp.broadcast_to(picks[None], (4, shots, count, capacity)), axis=3
    )
    keep = chosen[0].astype(jnp.int32) == index
    targets = jnp.where(keep, chosen[1].astype(jnp.int32), cells).reshape(shots, count * capacity)
    real_in = chosen[2].reshape(shots, count * capacity)
    imag_in = chosen[3].reshape(shots, count * capacity)
    live = keep.astype(jnp.float32).reshape(shots, count * capacity)

    def per_shot(idx, values):
        return jax.ops.segment_sum(values, idx, num_segments=cells + 1)[:cells]

    stacked = jnp.stack([live, real_in, imag_in], axis=-1)
    sums = jax.vmap(per_shot)(targets, stacked)
    sums = jnp.moveaxis(sums, -1, 0)
    weight = sums[0].reshape(shots, depth, height, width)
    pdata = sums[1:].reshape(2, shots, depth, height, width)
    plane_cells = height * width
    positions = (
        jnp.arange((depth + 2) * plane_cells, dtype=jnp.int32) + (index * depth - 1) * plane_cells
    )
    hit = (positions[None, :] == src_cell[:, None]).astype(jnp.float32)
    source_ext = (src_amp[:, :, None] * hit[None]).reshape(2, shots, depth + 2, height, width)
    source = source_ext[:, :, 1:-1]
    rhs = helmholtz(source_ext, coeff, lossy, -1.0) + PENALTY * pdata
    wavefield = jnp.zeros_like(rhs)
    applied = jnp.zeros_like(rhs)
    residual = rhs
    direction = rhs
    norm_now = squares(residual)
    for step in range(ITERS):
        extended = padded_2(direction, (("slab", 2),), 1)
        image = helmholtz(extended, coeff, lossy, 1.0)
        image_ext = padded_2(image, (("slab", 2),), 1)
        result = helmholtz(image_ext, coeff, lossy, -1.0) + PENALTY * weight[None] * direction
        image, forward_dir = (result, image)
        curve = lax.psum(inner(direction, image), "slab")
        alpha = expand(norm_now / curve)
        wavefield = wavefield + alpha * direction
        applied = applied + alpha * forward_dir
        residual = residual - alpha * image
        norm_next = squares(residual)
        direction = residual + expand(norm_next / norm_now) * direction
        norm_now = norm_next
    misfit = applied - source
    scaled = DAMPING * mask_f
    grad_r = -K_SQ * (wavefield[0] - scaled * wavefield[1])
    grad_i = -K_SQ * (wavefield[1] + scaled * wavefield[0])
    numer = jnp.sum(grad_r * misfit[0] + grad_i * misfit[1], axis=0)
    denom = jnp.sum(grad_r * grad_r + grad_i * grad_i, axis=0)
    updated = slowness - numer / (denom + REGULAR)
    return (wavefield, updated)


def solution(mesh):
    return jax.shard_map(
        local,
        mesh=mesh,
        in_specs=(
            P("slab", "groups", None),
            P("slab", "groups", None),
            P("groups"),
            P(None, "groups"),
            P("groups", "slab", None),
            P("groups", "slab"),
            P(None, "groups", "slab"),
        ),
        out_specs=(P(None, "groups", "slab", None, None), P("slab", "groups", None)),
        check_vma=False,
    )
```

profile of v0, /device:TPU:0, one launch (start us, length us, event | category | flops | bytes accessed | tf_op | source)
XLA Modules:
  0.0 1141.6 jit_solution(10896158645109192802)
XLA Ops:
  15.3 36.2 %all-gather.2.cloned.1.call-done = f32[4,8,8192]{2,1,0:T(8,128)} async-done(((f32[4,8,512]{2,1,0:T(8,128)}), f32[4,8,8192]{2,1,0:T(8,128)}) %all-gather.2.cloned.1.call-update) | async-done | bytes 1048592 | tf_op jit(solution)/shard_map/all_gather | solution.py:71
  53.3 6.4 sort_prefixfusion
  62.3 664.8 %gather_fusion = f32[49152]{0:T(1024)} fusion(f32[4,8,16,512]{3,1,2,0:T(8,128)S(1)} %bitcast.84, s32[49152]{0:T(1024)S(1)} %reshape.171), kind=kCustom, calls=%fused_computation | custom fusion | bytes 1179648 | tf_op jit(solution)/shard_map/jit(take_along_axis)/gather | solution.py:77
  730.8 8.2 sort.1
  739.3 4.0 copy.27
  743.4 180.4 %scatter_custom_fusion = f32[3,131080]{0,1:T(8,128)} fusion(s32[12288]{0:T(1024)S(1)} %get-tuple-element.6, f32[]{:T(128)} %constant.13.clone.1, f32[12288,3]{1,0:T(8,128)} %bitcast.89, s32[12288]{0:T(1024)S(1)} %broadcast_clamp_fusion), kind=kCustom, calls=%fused_computation.3 | custom fusion | flops 36864 | bytes 1573472
  923.8 34.8 %copy.25 = f32[3,131080]{1,0:T(4,128)} copy(f32[3,131080]{0,1:T(8,128)} %scatter_custom_fusion) | data formatting | bytes 3145920
  958.6 4.3 reshape.168
  969.3 5.8 collective-permute-start.1
  977.0 4.7 fusion.15
  984.5 7.2 collective-permute-start.3
  991.7 2.1 fusion.54
  995.9 2.0 stack.60
  999.8 3.4 multiply_reduce_fusion.1
  1003.2 33.8 %all-reduce.5 = (f32[8]{0:T(128)S(1)}, f32[8]{0:T(128)S(1)}) all-reduce(f32[8]{0:T(128)S(1)} %get-tuple-element.12, f32[8]{0:T(128)S(1)} %get-tuple-element.11), channel_id=1, replica_groups=mesh['groups'=2,'slab'=16] {'slab'}, use_global_device_ids=true, to_apply=%region_3.4 | all-reduce | flops 16 | bytes 128 | tf_op jit(solution)/shard_map/psum | solution.py:49
  1037.0 2.1 multiply_reduce_fusion
  1041.1 29.5 %psum.30 = f32[8]{0:T(128)S(1)} all-reduce(f32[8]{0:T(128)S(1)} %multiply_reduce_fusion), channel_id=1, replica_groups=mesh['groups'=2,'slab'=16] {'slab'}, use_global_device_ids=true, to_apply=%region_7.8 | all-reduce | flops 8 | bytes 64 | tf_op jit(solution)/shard_map/psum | solution.py:49
  1070.6 2.3 fusion.37
  1074.3 3.0 collective-permute-start.5
  1080.7 5.8 collective-permute-start.7
  1089.7 2.0 stack.65
  1093.6 2.5 fusion.39
  1096.2 34.1 %psum.31 = f32[8]{0:T(128)S(1)} all-reduce(f32[8]{0:T(128)S(1)} %fusion.39), channel_id=1, replica_groups=mesh['groups'=2,'slab'=16] {'slab'}, use_global_device_ids=true, to_apply=%region_9.10 | all-reduce | flops 8 | bytes 64 | tf_op jit(solution)/shard_map/psum | solution.py:113
  1130.3 3.1 add_subtract_fusion
  (101 shorter events, 44.0 us)
Async XLA Ops:
  7.2 44.3 %all-gather.2.cloned.1.call-start = ((), (), s32[]{:S(2)}) async-start(), calls=%async_computation | async-start | bytes 1114112 | tf_op jit(solution)/shard_map/all_gather | solution.py:71
  15.3 1055.3 %copy-start.3 = (f32[1,8,4,32,128]{4,3,2,1,0:T(8,128)}, f32[1,8,4,32,128]{4,3,2,1,0:T(8,128)S(1)}, u32[]{:S(2)}) copy-start(f32[1,8,4,32,128]{4,3,2,1,0:T(8,128)S(1)} %get-tuple-element.20) | copy-start | bytes 1572868
  51.5 10.8 copy-start
  59.7 0.6 copy-start.8
  59.8 0.6 copy-start.9
  958.6 7.3 copy-start.4
  964.4 1.2 copy-start.6
  964.5 1.4 copy-start.2
  966.2 1.0 copy-start.5
  968.0 9.0 collective-permute-start
  969.3 7.7 collective-permute-start.1
  983.2 10.7 collective-permute-start.2
  984.5 9.4 collective-permute-start.3
  1073.0 4.4 collective-permute-start.4
  1074.3 4.2 collective-permute-start.5
  1079.4 9.1 copy-start.1
  1079.4 7.2 collective-permute-start.6
  1080.7 6.9 collective-permute-start.7
  1093.6 39.8 %copy-start.10 = (f32[4,32,128]{2,1,0:T(8,128)S(1)}, f32[4,32,128]{2,1,0:T(8,128)}, u32[]{:S(2)}) copy-start(f32[4,32,128]{2,1,0:T(8,128)} %get-tuple-element.42) | copy-start | bytes 196612
  1096.2 37.5 %copy-start.11 = (f32[4,32,128]{2,1,0:T(8,128)S(1)}, f32[4,32,128]{2,1,0:T(8,128)}, u32[]{:S(2)}) copy-start(f32[4,32,128]{2,1,0:T(8,128)} %param.7) | copy-start | bytes 196612
  1133.4 1.0 copy-start.7
Sparse Core Ops, SparseCore 0:
  10.8 40.6 all-gather.1
where the time goes:
time: 1150 us; the launch traced here: 1140 us
  local copies, waits for them, and re-layouts  728 us (63%)
  other arithmetic  236 us (21%)
  blocking collectives  97.4 us (8%)
  waiting for transfers between devices  38.4 us (3%)
  starting transfers between devices  27.1 us (2%)
  between operations  15 us (1%)
    gather x3, local copies, waits for them, and re-layouts, local(): jnp.take_along_axis(grouped, jnp.broadcast_to(picks[None], (4, shots, cou...  667 us
    unnamed x7, other arithmetic  192 us
    psum x2, blocking collectives, squares(): return lax.psum(inner(residual, residual), 'slab')  63.3 us
    unnamed x30, local copies, waits for them, and re-layouts  44 us
    all_gather x1, waiting for transfers between devices, local(): table = lax.all_gather(packed, 'slab', axis=2, tiled=True)  36.2 us
    psum x1, blocking collectives, local(): curve = lax.psum(inner(direction, image), 'slab')  34.1 us
  transfers between devices with their start and end apart: 9, of which 3 were waited for; matrix products, arithmetic and copies ran while one was open for 1% of the time, Pallas kernels for 0%

commit v1 on v0

v1 whole, which is shorter than its diff:
```python
import functools

import jax
import jax.numpy as jnp
from jax import lax
from jax.experimental import pallas as pl
from jax.experimental.pallas import tpu as pltpu
from jax.sharding import PartitionSpec as P

K_SQ = 0.8
DAMPING = 0.6
PENALTY = 4.0
REGULAR = 0.5

LANES = 128
GROUP = 4
KINDS = 3
F32 = jnp.float32
BF16 = jnp.bfloat16
MESH = pl.DeviceIdType.MESH
NT = (((1,), (1,)), ((), ()))


def spread(row, rows):
    tile = jnp.broadcast_to(row, (16, row.shape[1])).astype(BF16)
    return jnp.concatenate([tile] * (rows // 16), axis=0)


def ramp(shape):
    return lax.broadcasted_iota(jnp.int32, shape, 0).astype(F32).astype(BF16)


def split(values):
    high = values.astype(BF16).astype(F32)
    return high, (values - high).astype(BF16).astype(F32)


def kernel(
    count, depth, height, slots,
    slow_ref, absorb_ref, cell_ref, amp_ref, own_ref, loc_ref, dat_ref,
    wave_ref, upd_ref,
    feats, ranks, send, recv, parts, weight, field, image, normal, rest, rest_image,
    halo, stat_a, all_a, stat_b, all_b, scal,
    route_s, route_r, sum_s, sum_r, halo_s, halo_r,
):
    me = lax.axis_index("slab")
    shots, block = own_ref.shape
    cells, width = slow_ref.shape
    dot = functools.partial(lax.dot_general, preferred_element_type=F32)

    def others(body):
        lax.fori_loop(1, count, lambda k, c: (body(k), c)[1], 0)

    def each_shot(body):
        lax.fori_loop(0, shots, lambda s, c: (body(s), c)[1], 0)

    barrier = pltpu.get_barrier_semaphore()

    def greet(k):
        pl.semaphore_signal(
            barrier, inc=1, device_id={"slab": lax.rem(me + k, count)}, device_id_type=MESH
        )

    others(greet)

    own, loc = own_ref[...], loc_ref[...]
    column = loc & (width - 1)
    real_hi, real_lo = split(dat_ref[0])
    imag_hi, imag_lo = split(dat_ref[1])
    zero = jnp.zeros((shots, block), F32)
    rows = [(loc - column).astype(F32), real_hi, imag_hi] + [zero] * 5
    rows += [(column + 1).astype(F32), real_lo, imag_lo] + [zero] * 5
    for at, row in enumerate(rows):
        feats[:, at, :] = row
    named = jnp.concatenate(
        [jnp.where(own == slab, 1.0, 0.0) for slab in range(count)], axis=0
    )
    first = lax.broadcasted_iota(jnp.int32, (block, block), 0)
    later = lax.broadcasted_iota(jnp.int32, (block, block), 1)
    before = jnp.where(first < later, 1.0, 0.0).astype(BF16)
    ahead = dot(named.astype(BF16), before, (((1,), (0,)), ((), ())))
    ranks[...] = jnp.where(named > 0.0, ahead, -1.0)

    slot = ramp((slots, block))
    one = jnp.ones((), BF16)
    nought = jnp.zeros((), BF16)

    def compact(s):
        values = feats[s].astype(BF16)
        for base in range(0, count, GROUP):
            picks = jnp.concatenate(
                [
                    jnp.where(
                        slot == spread(ranks[pl.ds(slab * shots + s, 1), :], slots), one, nought
                    )
                    for slab in range(base, base + GROUP)
                ],
                axis=0,
            )
            out = dot(values, picks, NT)
            out = out[:8] + out[8:]
            for i in range(GROUP):
                for kind in range(KINDS):
                    send[base + i, kind, pl.ds(s, 1), :] = out[
                        kind : kind + 1, i * slots : (i + 1) * slots
                    ]

    each_shot(compact)
    pl.semaphore_wait(barrier, count - 1)

    def routed(k):
        target = lax.rem(me + k, count)
        return pltpu.make_async_remote_copy(
            src_ref=send.at[target], dst_ref=recv.at[me],
            send_sem=route_s.at[k], recv_sem=route_r.at[k],
            device_id={"slab": target}, device_id_type=MESH,
        )

    def landed(k):
        source = lax.rem(me + count - k, count)
        return pltpu.make_async_remote_copy(
            src_ref=send.at[source], dst_ref=recv.at[source],
            send_sem=route_s.at[k], recv_sem=route_r.at[k],
            device_id={"slab": source}, device_id_type=MESH,
        )

    others(lambda k: routed(k).start())
    recv[me] = send[me]

    coeff = K_SQ * slow_ref[...]
    mask = absorb_ref[...].astype(F32)
    lossy = DAMPING * coeff * mask
    row_of = lax.broadcasted_iota(jnp.int32, (cells, width), 0)
    x_of = lax.broadcasted_iota(jnp.int32, (cells, width), 1)
    z_of = row_of // height + me * depth
    y_of = row_of % height
    at_top, at_bottom = y_of == 0, y_of == height - 1
    at_left, at_right = x_of == 0, x_of == width - 1

    def far(s):
        cell = cell_ref[s]
        plane = cell // (height * width)
        line = (cell // width) % height
        place = cell % width
        return jnp.abs(z_of - plane) + jnp.abs(y_of - line) + jnp.abs(x_of - place)

    def laplace(centre, low, high):
        beside = jnp.concatenate([centre[height:], high], axis=0)
        beside = beside + jnp.concatenate([low, centre[:-height]], axis=0)
        beside = beside + jnp.where(at_top, 0.0, pltpu.roll(centre, 1, 0))
        beside = beside + jnp.where(at_bottom, 0.0, pltpu.roll(centre, cells - 1, 0))
        beside = beside + jnp.where(at_left, 0.0, pltpu.roll(centre, 1, 1))
        beside = beside + jnp.where(at_right, 0.0, pltpu.roll(centre, width - 1, 1))
        return 6.0 * centre - beside

    def helmholtz(real, imag, low, high, sign):
        out_r = laplace(real, low[0], high[0]) - coeff * real + sign * lossy * imag
        out_i = laplace(imag, low[1], high[1]) - coeff * imag - sign * lossy * real
        return out_r, out_i

    for step in range(3):
        @pl.when(me == 0)
        def _(step=step):
            halo[step, 0] = jnp.zeros(halo.shape[2:], F32)

        @pl.when(me == count - 1)
        def _(step=step):
            halo[step, 1] = jnp.zeros(halo.shape[2:], F32)

    def edge(step, ref, s, side):
        target = me + 1 if side == 0 else me - 1
        at = cells - height if side == 0 else 0
        return pltpu.make_async_remote_copy(
            src_ref=ref.at[s, :, pl.ds(at, height), :], dst_ref=halo.at[step, side, s],
            send_sem=halo_s.at[step, side, s], recv_sem=halo_r.at[step, side, s],
            device_id={"slab": target}, device_id_type=MESH,
        )

    has = [me > 0, me < count - 1]

    def send_edges(step, ref, s):
        pl.when(has[1])(lambda: edge(step, ref, s, 0).start())
        pl.when(has[0])(lambda: edge(step, ref, s, 1).start())

    def wait_edges(step, ref, s):
        pl.when(has[0])(lambda: edge(step, ref, s, 0).wait_recv())
        pl.when(has[1])(lambda: edge(step, ref, s, 1).wait_recv())

    def sent_edges(step, ref, s):
        pl.when(has[1])(lambda: edge(step, ref, s, 0).wait_send())
        pl.when(has[0])(lambda: edge(step, ref, s, 1).wait_send())

    def along(values):
        return jnp.sum(values, axis=0, keepdims=True)

    def shared(which, ref, gathered, k):
        target = lax.rem(me + k, count)
        return pltpu.make_async_remote_copy(
            src_ref=ref, dst_ref=gathered.at[me],
            send_sem=sum_s.at[which, k], recv_sem=sum_r.at[which, k],
            device_id={"slab": target}, device_id_type=MESH,
        )

    def heard(which, ref, gathered, k):
        source = lax.rem(me + count - k, count)
        return pltpu.make_async_remote_copy(
            src_ref=ref, dst_ref=gathered.at[source],
            send_sem=sum_s.at[which, k], recv_sem=sum_r.at[which, k],
            device_id={"slab": source}, device_id_type=MESH,
        )

    def totals(gathered):
        return jnp.sum(jnp.sum(gathered[...], axis=0), axis=-1, keepdims=True)

    others(lambda k: landed(k).wait_recv())
    place = recv[:, 0].astype(jnp.int32) - 1
    parts[0] = (place >> (width.bit_length() - 1)).astype(F32)
    parts[1] = (place & (width - 1)).astype(F32)
    parts[2], parts[3] = split(recv[:, 1])
    parts[4], parts[5] = split(recv[:, 2])

    wide = GROUP * slots
    cell_row = ramp((cells, wide))
    cell_col = ramp((width, wide))

    def gather(s):
        total = None
        for base in range(0, count, GROUP):
            def line(kind, length):
                row = jnp.concatenate(
                    [parts[kind, base + i, pl.ds(s, 1), :] for i in range(GROUP)], axis=1
                )
                return spread(row, length)

            left = jnp.where(cell_row == line(0, cells), one, nought)
            same = cell_col == line(1, width)
            right = jnp.concatenate(
                [jnp.where(same, one, nought)]
                + [jnp.where(same, line(kind, width), nought) for kind in range(2, 6)],
                axis=0,
            )
            piece = dot(left, right, NT)
            total = piece if total is None else total + piece
        weight[s] = PENALTY * total[:, :width]
        data_r = total[:, width : 2 * width] + total[:, 2 * width : 3 * width]
        data_i = total[:, 3 * width : 4 * width] + total[:, 4 * width :]
        away = far(s)
        here = jnp.where(away == 0, 1.0, 0.0)
        lap = jnp.where(away == 0, 6.0, jnp.where(away == 1, -1.0, 0.0)) - coeff * here
        turn = lossy * here
        amp_r, amp_i = amp_ref[0, s], amp_ref[1, s]
        field[s, 0] = amp_r * lap - amp_i * turn + PENALTY * data_r
        field[s, 1] = amp_i * lap + amp_r * turn + PENALTY * data_i
        send_edges(0, field, s)

    each_shot(gather)

    def apply_first(s):
        wait_edges(0, field, s)
        r, i = field[s, 0], field[s, 1]
        out_r, out_i = helmholtz(r, i, halo[0, 0, s], halo[0, 1, s], 1.0)
        image[s, 0] = out_r
        image[s, 1] = out_i
        send_edges(1, image, s)
        size = r * r + i * i
        stat_a[0, pl.ds(s, 1), :] = along(size)
        stat_a[1, pl.ds(s, 1), :] = along(out_r * out_r + out_i * out_i + weight[s] * size)

    each_shot(apply_first)
    others(lambda k: shared(0, stat_a, all_a, k).start())
    all_a[me] = stat_a[...]

    def apply_back(s):
        wait_edges(1, image, s)
        out_r, out_i = helmholtz(image[s, 0], image[s, 1], halo[1, 0, s], halo[1, 1, s], -1.0)
        normal[s, 0] = out_r + weight[s] * field[s, 0]
        normal[s, 1] = out_i + weight[s] * field[s, 1]
        send_edges(2, normal, s)

    each_shot(apply_back)
    others(lambda k: heard(0, stat_a, all_a, k).wait_recv())
    norm, curve = totals(all_a)
    alpha = norm / curve
    scal[0] = jnp.broadcast_to(alpha, (shots, LANES))

    def apply_second(s):
        wait_edges(2, normal, s)
        step = scal[0, pl.ds(s, 1), :]
        r = field[s, 0] - step * normal[s, 0]
        i = field[s, 1] - step * normal[s, 1]
        low = halo[0, 0, s] - step[None] * halo[2, 0, s]
        high = halo[0, 1, s] - step[None] * halo[2, 1, s]
        out_r, out_i = helmholtz(r, i, low, high, 1.0)
        rest[s, 0] = r
        rest[s, 1] = i
        rest_image[s, 0] = out_r
        rest_image[s, 1] = out_i
        size = r * r + i * i
        stat_b[0, pl.ds(s, 1), :] = along(size)
        stat_b[1, pl.ds(s, 1), :] = along(out_r * out_r + out_i * out_i + weight[s] * size)
        stat_b[2, pl.ds(s, 1), :] = along(
            out_r * image[s, 0] + out_i * image[s, 1]
            + weight[s] * (r * field[s, 0] + i * field[s, 1])
        )

    each_shot(apply_second)
    others(lambda k: shared(1, stat_b, all_b, k).start())
    all_b[me] = stat_b[...]
    others(lambda k: heard(1, stat_b, all_b, k).wait_recv())
    following, own_curve, cross = totals(all_b)
    beta = following / norm
    second = following / (own_curve + beta * (2.0 * cross + beta * curve))
    scal[1] = jnp.broadcast_to(second, (shots, LANES))
    scal[2] = jnp.broadcast_to(alpha + second * beta, (shots, LANES))

    scaled = DAMPING * mask

    def finish(s, carry):
        numer, denom = carry
        on_rest = scal[1, pl.ds(s, 1), :]
        on_field = scal[2, pl.ds(s, 1), :]
        here = jnp.where(far(s) == 0, 1.0, 0.0)
        u_r = on_field * field[s, 0] + on_rest * rest[s, 0]
        u_i = on_field * field[s, 1] + on_rest * rest[s, 1]
        wave_ref[0, s] = u_r
        wave_ref[1, s] = u_i
        mis_r = on_field * image[s, 0] + on_rest * rest_image[s, 0] - amp_ref[0, s] * here
        mis_i = on_field * image[s, 1] + on_rest * rest_image[s, 1] - amp_ref[1, s] * here
        grad_r = -K_SQ * (u_r - scaled * u_i)
        grad_i = -K_SQ * (u_i + scaled * u_r)
        return (
            numer + grad_r * mis_r + grad_i * mis_i,
            denom + grad_r * grad_r + grad_i * grad_i,
        )

    empty = jnp.zeros((cells, width), F32)
    numer, denom = lax.fori_loop(0, shots, finish, (empty, empty))
    upd_ref[...] = slow_ref[...] - numer / (denom + REGULAR)

    def drain(s):
        sent_edges(0, field, s)
        sent_edges(1, image, s)
        sent_edges(2, normal, s)

    each_shot(drain)

    def drain_small(k):
        routed(k).wait_send()
        shared(0, stat_a, all_a, k).wait_send()
        shared(1, stat_b, all_b, k).wait_send()

    others(drain_small)


def local(slowness, absorbing, src_cell, src_amp, rec_slab, rec_local, rec_data):
    count = lax.axis_size("slab")
    depth, height, width = slowness.shape
    cells = depth * height
    shots, block = rec_local.shape
    capacity = 3 * block // count
    slots = -(-capacity // LANES) * LANES
    vmem = pl.BlockSpec(memory_space=pltpu.VMEM)
    smem = pl.BlockSpec(memory_space=pltpu.SMEM)
    pair = pltpu.VMEM((shots, 2, cells, width), F32)
    dma = pltpu.SemaphoreType.DMA
    wavefield, updated = pl.pallas_call(
        functools.partial(kernel, count, depth, height, slots),
        out_shape=(
            jax.ShapeDtypeStruct((2, shots, cells, width), F32),
            jax.ShapeDtypeStruct((cells, width), F32),
        ),
        in_specs=[vmem, vmem, smem, smem, vmem, vmem, vmem],
        out_specs=(vmem, vmem),
        scratch_shapes=[
            pltpu.VMEM((shots, 16, block), F32),
            pltpu.VMEM((count * shots, block), F32),
            pltpu.VMEM((count, KINDS, shots, slots), F32),
            pltpu.VMEM((count, KINDS, shots, slots), F32),
            pltpu.VMEM((6, count, shots, slots), F32),
            pltpu.VMEM((shots, cells, width), F32),
            pair, pair, pair, pair, pair,
            pltpu.VMEM((3, 2, shots, 2, height, width), F32),
            pltpu.VMEM((2, shots, LANES), F32),
            pltpu.VMEM((count, 2, shots, LANES), F32),
            pltpu.VMEM((3, shots, LANES), F32),
            pltpu.VMEM((count, 3, shots, LANES), F32),
            pltpu.VMEM((3, shots, LANES), F32),
            dma((count,)), dma((count,)),
            dma((2, count)), dma((2, count)),
            dma((3, 2, shots)), dma((3, 2, shots)),
        ],
        compiler_params=pltpu.CompilerParams(
            collective_id=0, has_side_effects=True, vmem_limit_bytes=48 * 1024 * 1024
        ),
    )(
        slowness.reshape(cells, width),
        absorbing.reshape(cells, width),
        src_cell,
        src_amp,
        rec_slab.reshape(shots, block),
        rec_local,
        rec_data,
    )
    return (
        wavefield.reshape(2, shots, depth, height, width),
        updated.reshape(depth, height, width),
    )


def solution(mesh):
    return jax.shard_map(
        local,
        mesh=mesh,
        in_specs=(
            P("slab", "groups", None),
            P("slab", "groups", None),
            P("groups"),
            P(None, "groups"),
            P("groups", "slab", None),
            P("groups", "slab"),
            P(None, "groups", "slab"),
        ),
        out_specs=(P(None, "groups", "slab", None, None), P("slab", "groups", None)),
        check_vma=False,
    )
```

time: 1150 us -> 52.5 us (0.05)
  local copies, waits for them, and re-layouts: 728 us -> 5.41 us
  other arithmetic: 236 us -> 0 us
  blocking collectives: 97.4 us -> 0 us
  Pallas kernels: 0 us -> 46 us
  waiting for transfers between devices: 38.4 us -> 0 us
  starting transfers between devices: 27.1 us -> 0 us
  between operations: 15 us -> 0.65 us
    gather x3 -> x0, local copies, waits for them, and re-layouts: 667 us -> none  [local(): jnp.take_along_axis(grouped, jnp.broadcast_to(picks[None], (4, shots, cou...]
    unnamed x7 -> x0, other arithmetic: 192 us -> none
    psum x3 -> x0, blocking collectives: 97.4 us -> none  [the longest x2 63.3 us: squares(): return lax.psum(inner(residual, residual), 'slab')]
    pallas_call x0 -> x1, Pallas kernels: none -> 46 us  [local(): pl.pallas_call(functools.partial(kernel, count, depth, height, slots), ou...]
    unnamed x30 -> x15, local copies, waits for them, and re-layouts: 44 us -> 5.41 us
    all_gather x1 -> x0, waiting for transfers between devices: 36.2 us -> none  [local(): table = lax.all_gather(packed, 'slab', axis=2, tiled=True)]
    ppermute x8 -> x0, starting transfers between devices: 27 us -> none  [the longest x4 21.9 us: padded_2(): lax.ppermute(lax.slice_in_dim(block, block.shape[dim] - width, None, axis...]
    another operation x9 -> x0, local copies, waits for them, and re-layouts: 13.8 us -> none  [the longest x6 9.6 us: helmholtz(): return jnp.stack([real_part, imag_part])]
  transfers between devices with their start and end apart: 9 -> 0, of which waited for: 3 -> 0; matrix products, arithmetic and copies ran while one was open for 1% -> 0% of each run, Pallas kernels for 0% -> 0%
where the time goes in v1:
time: 52.5 us; the launch traced here: 52.1 us
  Pallas kernels  46 us (88%)
  local copies, waits for them, and re-layouts  5.41 us (10%)
  between operations  0.65 us (1%)
    pallas_call x1, Pallas kernels, local(): pl.pallas_call(functools.partial(kernel, count, depth, height, slots), ou...  46 us
    unnamed x15, local copies, waits for them, and re-layouts  5.41 us

profile of v1, /device:TPU:0, one launch (start us, length us, event | category | flops | bytes accessed | tf_op | source)
XLA Modules:
  0.0 52.1 jit_solution(5939348967867820018)
XLA Ops:
  0.6 0.0 copy-start.2
  0.6 0.7 %copy.11 = s32[8,512,1]{1,0,2:T(8,128)S(1)} copy(s32[8,512,1]{1,2,0:T(1,128)} %param.11) | data formatting | bytes 32768
  1.4 0.0 copy-start.4
  1.4 0.0 copy-start.5
  1.4 0.0 copy-done.2
  1.4 0.7 %copy-done.4 = f32[2,8]{1,0:T(2,128)S(1)} copy-done((f32[2,8]{1,0:T(2,128)S(1)}, f32[2,8]{1,0:T(2,128)}, u32[]{:S(2)}) %copy-start.4) | copy-done | bytes 88
  2.0 0.0 copy-done.5
  2.1 0.0 copy-start
  2.1 0.8 %copy-done = f32[4,32,128]{2,1,0:T(8,128)S(1)} copy-done((f32[4,32,128]{2,1,0:T(8,128)S(1)}, f32[4,32,128]{2,1,0:T(8,128)}, u32[]{:S(2)}) %copy-start) | copy-done | bytes 65560
  2.9 0.0 copy-start.1
  2.9 0.8 %copy-done.1 = s32[4,32,128]{2,1,0:T(8,128)S(1)} copy-done((s32[4,32,128]{2,1,0:T(8,128)S(1)}, s32[4,32,128]{2,1,0:T(8,128)}, u32[]{:S(2)}) %copy-start.1) | copy-done | bytes 65560
  3.7 0.0 copy-start.3
  3.7 0.7 %copy-done.3 = s32[8,512]{1,0:T(8,128)S(1)} copy-done((s32[8,512]{1,0:T(8,128)S(1)}, s32[8,512]{1,0:T(8,128)}, u32[]{:S(2)}) %copy-start.3) | copy-done | bytes 16408
  4.4 46.0 %shard_map.86 = (f32[2,8,128,128]{3,2,1,0:T(8,128)S(1)}, f32[128,128]{1,0:T(8,128)S(1)}) custom-call(f32[128,128]{1,0:T(8,128)S(1)} %bitcast.8, s32[128,128]{1,0:T(8,128)S(1)} %bitcast.9, s32[8]{0:T(128)S(1)} %copy-done.5, f32[2,8]{1,0:T(2,128)S(1)} %copy-done.4, s32[8,512]{1,0:T(8,128)S(1)} %bitcast.10, s32[8,512]{1,0:T(8,128)S(1)} %copy-done.3, ...), custom_call_target="tpu_custom_call" | custom-call | tf_op jit(solution)/shard_map/pallas_call | solution.py:366
  50.5 1.0 %copy.14 = f32[2,8,4,32,128]{4,3,2,1,0:T(8,128)} copy(f32[2,8,4,32,128]{4,3,2,1,0:T(8,128)S(1)} %bitcast.7) | data formatting | bytes 2097152
  51.5 0.6 %copy.15 = f32[4,32,128]{2,1,0:T(8,128)} copy(f32[4,32,128]{2,1,0:T(8,128)S(1)} %bitcast.11) | data formatting | bytes 131072
Async XLA Ops:
  0.6 0.8 %copy-start.2 = (f32[2,8,512]{2,1,0:T(8,128)S(1)}, f32[2,8,512]{2,1,0:T(8,128)}, u32[]{:S(2)}) copy-start(f32[2,8,512]{2,1,0:T(8,128)} %dat_ref.1) | copy-start | bytes 98308
  1.4 0.7 %copy-start.4 = (f32[2,8]{1,0:T(2,128)S(1)}, f32[2,8]{1,0:T(2,128)}, u32[]{:S(2)}) copy-start(f32[2,8]{1,0:T(2,128)} %amp_ref.1) | copy-start | bytes 196
  1.4 0.7 %copy-start.5 = (s32[8]{0:T(128)S(1)}, s32[8]{0:T(128)}, u32[]{:S(2)}) copy-start(s32[8]{0:T(128)} %cell_ref.1) | copy-start | bytes 100
  2.1 0.8 %copy-start = (f32[4,32,128]{2,1,0:T(8,128)S(1)}, f32[4,32,128]{2,1,0:T(8,128)}, u32[]{:S(2)}) copy-start(f32[4,32,128]{2,1,0:T(8,128)} %param.7) | copy-start | bytes 196612
  2.9 0.8 %copy-start.1 = (s32[4,32,128]{2,1,0:T(8,128)S(1)}, s32[4,32,128]{2,1,0:T(8,128)}, u32[]{:S(2)}) copy-start(s32[4,32,128]{2,1,0:T(8,128)} %param.8) | copy-start | bytes 196612
  3.7 0.7 %copy-start.3 = (s32[8,512]{1,0:T(8,128)S(1)}, s32[8,512]{1,0:T(8,128)}, u32[]{:S(2)}) copy-start(s32[8,512]{1,0:T(8,128)} %loc_ref.1) | copy-start | bytes 49156

commit v2 on v1

--- a/solution.py
+++ b/solution.py
@@ -37,14 +37,15 @@
 
 def kernel(
     count, depth, height, slots,
-    slow_ref, absorb_ref, cell_ref, amp_ref, own_ref, loc_ref, dat_ref,
-    wave_ref, upd_ref,
+    slow_in, absorb_in, cell_ref, amp_ref, own_in, loc_in, dat_in,
+    wave_out, upd_ref,
+    wave_ref, slow_ref, absorb_ref, own_ref, loc_ref, dat_ref, sums,
     feats, ranks, send, recv, parts, weight, field, image, normal, rest, rest_image,
-    halo, stat_a, all_a, stat_b, all_b, scal,
-    route_s, route_r, sum_s, sum_r, halo_s, halo_r,
+    halo, stat_a, note_a, all_a, stat_b, note_b, all_b, scal,
+    load_s, store_s, route_s, route_r, sum_s, sum_r, halo_s, halo_r,
 ):
     me = lax.axis_index("slab")
-    shots, block = own_ref.shape
+    shots, block = loc_ref.shape
     cells, width = slow_ref.shape
     dot = functools.partial(lax.dot_general, preferred_element_type=F32)
 
@@ -61,9 +62,20 @@
             barrier, inc=1, device_id={"slab": lax.rem(me + k, count)}, device_id_type=MESH
         )
 
+    loads = [
+        pltpu.make_async_copy(source, target, load_s.at[at])
+        for at, (source, target) in enumerate(
+            [(own_in, own_ref), (loc_in, loc_ref), (dat_in, dat_ref),
+             (slow_in, slow_ref), (absorb_in, absorb_ref)]
+        )
+    ]
+    for load in loads:
+        load.start()
     others(greet)
-
-    own, loc = own_ref[...], loc_ref[...]
+    for load in loads[:3]:
+        load.wait()
+
+    own, loc = own_ref[:, 0, :], loc_ref[...]
     column = loc & (width - 1)
     real_hi, real_lo = split(dat_ref[0])
     imag_hi, imag_lo = split(dat_ref[1])
@@ -111,21 +123,15 @@
     def routed(k):
         target = lax.rem(me + k, count)
         return pltpu.make_async_remote_copy(
-            src_ref=send.at[target], dst_ref=recv.at[me],
+            src_ref=send.at[target], dst_ref=recv.at[k],
             send_sem=route_s.at[k], recv_sem=route_r.at[k],
             device_id={"slab": target}, device_id_type=MESH,
         )
 
-    def landed(k):
-        source = lax.rem(me + count - k, count)
-        return pltpu.make_async_remote_copy(
-            src_ref=send.at[source], dst_ref=recv.at[source],
-            send_sem=route_s.at[k], recv_sem=route_r.at[k],
-            device_id={"slab": source}, device_id_type=MESH,
-        )
-
     others(lambda k: routed(k).start())
-    recv[me] = send[me]
+    recv[0] = send[me]
+    for load in loads[3:]:
+        load.wait()
 
     coeff = K_SQ * slow_ref[...]
     mask = absorb_ref[...].astype(F32)
@@ -193,54 +199,57 @@
     def along(values):
         return jnp.sum(values, axis=0, keepdims=True)
 
-    def shared(which, ref, gathered, k):
-        target = lax.rem(me + k, count)
+    def shared(which, note, gathered, k):
         return pltpu.make_async_remote_copy(
-            src_ref=ref, dst_ref=gathered.at[me],
+            src_ref=note, dst_ref=gathered.at[k],
             send_sem=sum_s.at[which, k], recv_sem=sum_r.at[which, k],
-            device_id={"slab": target}, device_id_type=MESH,
-        )
-
-    def heard(which, ref, gathered, k):
-        source = lax.rem(me + count - k, count)
-        return pltpu.make_async_remote_copy(
-            src_ref=ref, dst_ref=gathered.at[source],
-            send_sem=sum_s.at[which, k], recv_sem=sum_r.at[which, k],
-            device_id={"slab": source}, device_id_type=MESH,
-        )
-
-    def totals(gathered):
-        return jnp.sum(jnp.sum(gathered[...], axis=0), axis=-1, keepdims=True)
-
-    others(lambda k: landed(k).wait_recv())
-    place = recv[:, 0].astype(jnp.int32) - 1
-    parts[0] = (place >> (width.bit_length() - 1)).astype(F32)
-    parts[1] = (place & (width - 1)).astype(F32)
-    parts[2], parts[3] = split(recv[:, 1])
-    parts[4], parts[5] = split(recv[:, 2])
+            device_id={"slab": lax.rem(me + k, count)}, device_id_type=MESH,
+        )
+
+    def diagonal(values):
+        lane = lax.broadcasted_iota(jnp.int32, values.shape, 1)
+        return jnp.where(lane == lax.broadcasted_iota(jnp.int32, values.shape, 0), values, 0.0)
+
+    def share(which, stat, note, gathered):
+        kinds = stat.shape[0] * shots
+        own_sums = jnp.sum(stat[...].reshape(kinds, LANES), axis=1, keepdims=True)
+        note[...] = along(diagonal(jnp.broadcast_to(own_sums, (kinds, LANES))))
+        others(lambda k: shared(which, note, gathered, k).start())
+        gathered[0] = note[...]
+
+    def totals(which, stat, note, gathered):
+        others(lambda k: shared(which, note, gathered, k).wait_recv())
+        kinds = stat.shape[0] * shots
+        line = jnp.sum(gathered[...], axis=0)
+        column = jnp.sum(
+            diagonal(jnp.broadcast_to(line, (kinds, LANES))), axis=1, keepdims=True
+        )
+        return [column[at : at + shots] for at in range(0, kinds, shots)]
 
     wide = GROUP * slots
     cell_row = ramp((cells, wide))
     cell_col = ramp((width, wide))
 
-    def gather(s):
-        total = None
-        for base in range(0, count, GROUP):
-            def line(kind, length):
-                row = jnp.concatenate(
-                    [parts[kind, base + i, pl.ds(s, 1), :] for i in range(GROUP)], axis=1
-                )
-                return spread(row, length)
-
-            left = jnp.where(cell_row == line(0, cells), one, nought)
-            same = cell_col == line(1, width)
-            right = jnp.concatenate(
-                [jnp.where(same, one, nought)]
-                + [jnp.where(same, line(kind, width), nought) for kind in range(2, 6)],
-                axis=0,
+    def gather(base, s):
+        def line(kind, length):
+            row = jnp.concatenate(
+                [parts[kind, base + i, pl.ds(s, 1), :] for i in range(GROUP)], axis=1
             )
-            piece = dot(left, right, NT)
-            total = piece if total is None else total + piece
+            return spread(row, length)
+
+        left = jnp.where(cell_row == line(0, cells), one, nought)
+        same = cell_col == line(1, width)
+        right = jnp.concatenate(
+            [jnp.where(same, one, nought)]
+            + [jnp.where(same, line(kind, width), nought) for kind in range(2, 6)],
+            axis=0,
+        )
+        total = dot(left, right, NT)
+        if base > 0:
+            total = sums[s] + total
+        if base + GROUP < count:
+            sums[s] = total
+            return
         weight[s] = PENALTY * total[:, :width]
         data_r = total[:, width : 2 * width] + total[:, 2 * width : 3 * width]
         data_i = total[:, 3 * width : 4 * width] + total[:, 4 * width :]
@@ -253,7 +262,16 @@
         field[s, 1] = amp_i * lap + amp_r * turn + PENALTY * data_i
         send_edges(0, field, s)
 
-    each_shot(gather)
+    for base in range(0, count, GROUP):
+        for k in range(max(base, 1), base + GROUP):
+            routed(k).wait_recv()
+        part = pl.ds(base, GROUP)
+        place = recv[part, 0].astype(jnp.int32) - 1
+        parts[0, part] = (place >> (width.bit_length() - 1)).astype(F32)
+        parts[1, part] = (place & (width - 1)).astype(F32)
+        parts[2, part], parts[3, part] = split(recv[part, 1])
+        parts[4, part], parts[5, part] = split(recv[part, 2])
+        each_shot(functools.partial(gather, base))
 
     def apply_first(s):
         wait_edges(0, field, s)
@@ -267,8 +285,7 @@
         stat_a[1, pl.ds(s, 1), :] = along(out_r * out_r + out_i * out_i + weight[s] * size)
 
     each_shot(apply_first)
-    others(lambda k: shared(0, stat_a, all_a, k).start())
-    all_a[me] = stat_a[...]
+    share(0, stat_a, note_a, all_a)
 
     def apply_back(s):
         wait_edges(1, image, s)
@@ -278,8 +295,7 @@
         send_edges(2, normal, s)
 
     each_shot(apply_back)
-    others(lambda k: heard(0, stat_a, all_a, k).wait_recv())
-    norm, curve = totals(all_a)
+    norm, curve = totals(0, stat_a, note_a, all_a)
     alpha = norm / curve
     scal[0] = jnp.broadcast_to(alpha, (shots, LANES))
 
@@ -304,16 +320,17 @@
         )
 
     each_shot(apply_second)
-    others(lambda k: shared(1, stat_b, all_b, k).start())
-    all_b[me] = stat_b[...]
-    others(lambda k: heard(1, stat_b, all_b, k).wait_recv())
-    following, own_curve, cross = totals(all_b)
+    share(1, stat_b, note_b, all_b)
+    following, own_curve, cross = totals(1, stat_b, note_b, all_b)
     beta = following / norm
     second = following / (own_curve + beta * (2.0 * cross + beta * curve))
     scal[1] = jnp.broadcast_to(second, (shots, LANES))
     scal[2] = jnp.broadcast_to(alpha + second * beta, (shots, LANES))
 
     scaled = DAMPING * mask
+
+    def store(s):
+        return pltpu.make_async_copy(wave_ref.at[:, s], wave_out.at[:, s], store_s.at[s])
 
     def finish(s, carry):
         numer, denom = carry
@@ -324,6 +341,7 @@
         u_i = on_field * field[s, 1] + on_rest * rest[s, 1]
         wave_ref[0, s] = u_r
         wave_ref[1, s] = u_i
+        store(s).start()
         mis_r = on_field * image[s, 0] + on_rest * rest_image[s, 0] - amp_ref[0, s] * here
         mis_i = on_field * image[s, 1] + on_rest * rest_image[s, 1] - amp_ref[1, s] * here
         grad_r = -K_SQ * (u_r - scaled * u_i)
@@ -341,13 +359,14 @@
         sent_edges(0, field, s)
         sent_edges(1, image, s)
         sent_edges(2, normal, s)
+        store(s).wait()
 
     each_shot(drain)
 
     def drain_small(k):
         routed(k).wait_send()
-        shared(0, stat_a, all_a, k).wait_send()
-        shared(1, stat_b, all_b, k).wait_send()
+        shared(0, note_a, all_a, k).wait_send()
+        shared(1, note_b, all_b, k).wait_send()
 
     others(drain_small)
 
@@ -360,6 +379,7 @@
     capacity = 3 * block // count
     slots = -(-capacity // LANES) * LANES
     vmem = pl.BlockSpec(memory_space=pltpu.VMEM)
+    hbm = pl.BlockSpec(memory_space=pltpu.HBM)
     smem = pl.BlockSpec(memory_space=pltpu.SMEM)
     pair = pltpu.VMEM((shots, 2, cells, width), F32)
     dma = pltpu.SemaphoreType.DMA
@@ -369,9 +389,16 @@
             jax.ShapeDtypeStruct((2, shots, cells, width), F32),
             jax.ShapeDtypeStruct((cells, width), F32),
         ),
-        in_specs=[vmem, vmem, smem, smem, vmem, vmem, vmem],
-        out_specs=(vmem, vmem),
+        in_specs=[hbm, hbm, smem, smem, hbm, hbm, hbm],
+        out_specs=(hbm, vmem),
         scratch_shapes=[
+            pltpu.VMEM((2, shots, cells, width), F32),
+            pltpu.VMEM((cells, width), F32),
+            pltpu.VMEM((cells, width), jnp.int32),
+            pltpu.VMEM((shots, 1, block), jnp.int32),
+            pltpu.VMEM((shots, block), jnp.int32),
+            pltpu.VMEM((2, shots, block), F32),
+            pltpu.VMEM((shots, cells, 5 * width), F32),
             pltpu.VMEM((shots, 16, block), F32),
             pltpu.VMEM((count * shots, block), F32),
             pltpu.VMEM((count, KINDS, shots, slots), F32),
@@ -381,23 +408,25 @@
             pair, pair, pair, pair, pair,
             pltpu.VMEM((3, 2, shots, 2, height, width), F32),
             pltpu.VMEM((2, shots, LANES), F32),
-            pltpu.VMEM((count, 2, shots, LANES), F32),
+            pltpu.VMEM((1, LANES), F32),
+            pltpu.VMEM((count, 1, LANES), F32),
             pltpu.VMEM((3, shots, LANES), F32),
-            pltpu.VMEM((count, 3, shots, LANES), F32),
+            pltpu.VMEM((1, LANES), F32),
+            pltpu.VMEM((count, 1, LANES), F32),
             pltpu.VMEM((3, shots, LANES), F32),
-            dma((count,)), dma((count,)),
+            dma((5,)), dma((shots,)), dma((count,)), dma((count,)),
             dma((2, count)), dma((2, count)),
             dma((3, 2, shots)), dma((3, 2, shots)),
         ],
         compiler_params=pltpu.CompilerParams(
-            collective_id=0, has_side_effects=True, vmem_limit_bytes=48 * 1024 * 1024
+            collective_id=0, has_side_effects=True, vmem_limit_bytes=60 * 1024 * 1024
         ),
     )(
         slowness.reshape(cells, width),
         absorbing.reshape(cells, width),
         src_cell,
         src_amp,
-        rec_slab.reshape(shots, block),
+        rec_slab.reshape(shots, 1, block),
         rec_local,
         rec_data,
     )

time: 52.5 us -> 54 us (1.029)
  Pallas kernels: 46 us -> 50.1 us
  local copies, waits for them, and re-layouts: 5.41 us -> 2.95 us
    pallas_call x1, Pallas kernels: 46 us -> 50.1 us  [local(): pl.pallas_call(functools.partial(kernel, count, depth, height, slots), ou...]
    unnamed x15 -> x4, local copies, waits for them, and re-layouts: 5.41 us -> 2.95 us
where the time goes in v2:
time: 54 us; the launch traced here: 53.7 us
  Pallas kernels  50.1 us (93%)
  local copies, waits for them, and re-layouts  2.95 us (5%)
  between operations  0.65 us (1%)
    pallas_call x1, Pallas kernels, local(): pl.pallas_call(functools.partial(kernel, count, depth, height, slots), ou...  50.1 us
    unnamed x4, local copies, waits for them, and re-layouts  2.95 us

profile of v2, /device:TPU:0, one launch (start us, length us, event | category | flops | bytes accessed | tf_op | source)
XLA Modules:
  0.0 53.7 jit_solution(742527138385261997)
XLA Ops:
  0.6 50.1 %shard_map.86 = (f32[2,8,128,128]{3,2,1,0:T(8,128)}, f32[128,128]{1,0:T(8,128)}) custom-call(f32[128,128]{1,0:T(8,128)} %bitcast.6, s32[128,128]{1,0:T(8,128)} %bitcast.7, s32[8]{0:T(128)} %cell_ref.1, f32[2,8]{1,0:T(2,128)} %amp_ref.1, s32[8,1,512]{2,1,0:T(1,128)} %bitcast.9, s32[8,512]{1,0:T(8,128)} %loc_in.1, f32[2,8,512]{2,1,0:T(8,128)} %dat_in.1), custom_call_target="tpu_custom_call" | custom-call | tf_op jit(solution)/shard_map/pallas_call | solution.py:386
  50.8 0.0 copy-start
  50.8 2.3 %copy.11 = f32[2,8,4,32,128]{4,3,2,1,0:T(8,128)} copy(f32[2,8,4,32,128]{4,3,2,1,0:T(8,128)} %bitcast.5) | data formatting | bytes 2097152
  53.1 0.0 copy-done
  53.1 0.6 %copy.12 = f32[4,32,128]{2,1,0:T(8,128)} copy(f32[4,32,128]{2,1,0:T(8,128)S(1)} %bitcast.8) | data formatting | bytes 131072
Async XLA Ops:
  50.8 2.3 %copy-start = (f32[128,128]{1,0:T(8,128)S(1)}, f32[128,128]{1,0:T(8,128)}, u32[]{:S(2)}) copy-start(f32[128,128]{1,0:T(8,128)} %get-tuple-element.5) | copy-start | bytes 196612

commit v3 on v2

--- a/solution.py
+++ b/solution.py
@@ -13,7 +13,7 @@
 REGULAR = 0.5
 
 LANES = 128
-GROUP = 4
+SPAN = 768
 KINDS = 3
 F32 = jnp.float32
 BF16 = jnp.bfloat16
@@ -36,7 +36,7 @@
 
 
 def kernel(
-    count, depth, height, slots,
+    count, depth, height, slots, capacity,
     slow_in, absorb_in, cell_ref, amp_ref, own_in, loc_in, dat_in,
     wave_out, upd_ref,
     wave_ref, slow_ref, absorb_ref, own_ref, loc_ref, dat_ref, sums,
@@ -79,9 +79,8 @@
     column = loc & (width - 1)
     real_hi, real_lo = split(dat_ref[0])
     imag_hi, imag_lo = split(dat_ref[1])
-    zero = jnp.zeros((shots, block), F32)
-    rows = [(loc - column).astype(F32), real_hi, imag_hi] + [zero] * 5
-    rows += [(column + 1).astype(F32), real_lo, imag_lo] + [zero] * 5
+    rows = [(loc - column).astype(F32), (column + 1).astype(F32)]
+    rows += [real_hi, real_lo, imag_hi, imag_lo]
     for at, row in enumerate(rows):
         feats[:, at, :] = row
     named = jnp.concatenate(
@@ -91,31 +90,32 @@
     later = lax.broadcasted_iota(jnp.int32, (block, block), 1)
     before = jnp.where(first < later, 1.0, 0.0).astype(BF16)
     ahead = dot(named.astype(BF16), before, (((1,), (0,)), ((), ())))
-    ranks[...] = jnp.where(named > 0.0, ahead, -1.0)
+    chosen = named * ahead
+    rank = chosen[:shots]
+    for slab in range(1, count):
+        rank = rank + chosen[slab * shots : (slab + 1) * shots]
+    ranks[...] = rank
 
     slot = ramp((slots, block))
+    slab_of = ramp((count, block))
     one = jnp.ones((), BF16)
     nought = jnp.zeros((), BF16)
 
     def compact(s):
-        values = feats[s].astype(BF16)
-        for base in range(0, count, GROUP):
-            picks = jnp.concatenate(
-                [
-                    jnp.where(
-                        slot == spread(ranks[pl.ds(slab * shots + s, 1), :], slots), one, nought
-                    )
-                    for slab in range(base, base + GROUP)
-                ],
-                axis=0,
-            )
-            out = dot(values, picks, NT)
-            out = out[:8] + out[8:]
-            for i in range(GROUP):
-                for kind in range(KINDS):
-                    send[base + i, kind, pl.ds(s, 1), :] = out[
-                        kind : kind + 1, i * slots : (i + 1) * slots
-                    ]
+        right = jnp.where(slot == spread(ranks[pl.ds(s, 1), :], slots), one, nought)
+        mine = slab_of == spread(own_ref[s].astype(F32), count)
+        left = jnp.concatenate(
+            [
+                jnp.where(mine, spread(feats[s, at : at + 1, :], count), nought)
+                for at in range(2 * KINDS)
+            ],
+            axis=0,
+        )
+        out = dot(left, right, NT)
+        for kind in range(KINDS):
+            at = 2 * kind * count
+            value = out[at : at + count] + out[at + count : at + 2 * count]
+            send[:, kind, pl.ds(s, 1), :] = value.reshape(count, 1, slots)
 
     each_shot(compact)
     pl.semaphore_wait(barrier, count - 1)
@@ -226,33 +226,37 @@
         )
         return [column[at : at + shots] for at in range(0, kinds, shots)]
 
-    wide = GROUP * slots
-    cell_row = ramp((cells, wide))
-    cell_col = ramp((width, wide))
+    group = min(count, SPAN // capacity)
+    wide = group * capacity
+    half = cells // 2
+    cell_row = ramp((half, wide))
+    cell_col = ramp((2 * width, wide))
 
     def gather(base, s):
         def line(kind, length):
-            row = jnp.concatenate(
-                [parts[kind, base + i, pl.ds(s, 1), :] for i in range(GROUP)], axis=1
-            )
-            return spread(row, length)
-
-        left = jnp.where(cell_row == line(0, cells), one, nought)
-        same = cell_col == line(1, width)
-        right = jnp.concatenate(
+            return spread(parts[base // group, kind, pl.ds(s, 1), :], length)
+
+        right = jnp.where(cell_col == line(1, 2 * width), one, nought)
+        same = cell_row == line(0, half)
+        left = jnp.concatenate(
             [jnp.where(same, one, nought)]
-            + [jnp.where(same, line(kind, width), nought) for kind in range(2, 6)],
+            + [jnp.where(same, line(kind, half), nought) for kind in range(2, 6)],
             axis=0,
         )
         total = dot(left, right, NT)
         if base > 0:
             total = sums[s] + total
-        if base + GROUP < count:
+        if base + group < count:
             sums[s] = total
             return
-        weight[s] = PENALTY * total[:, :width]
-        data_r = total[:, width : 2 * width] + total[:, 2 * width : 3 * width]
-        data_i = total[:, 3 * width : 4 * width] + total[:, 4 * width :]
+
+        def field_of(at):
+            piece = total[at * half : (at + 1) * half]
+            return jnp.concatenate([piece[:, :width], piece[:, width:]], axis=0)
+
+        weight[s] = PENALTY * field_of(0)
+        data_r = field_of(1) + field_of(2)
+        data_i = field_of(3) + field_of(4)
         away = far(s)
         here = jnp.where(away == 0, 1.0, 0.0)
         lap = jnp.where(away == 0, 6.0, jnp.where(away == 1, -1.0, 0.0)) - coeff * here
@@ -262,15 +266,23 @@
         field[s, 1] = amp_i * lap + amp_r * turn + PENALTY * data_i
         send_edges(0, field, s)
 
-    for base in range(0, count, GROUP):
-        for k in range(max(base, 1), base + GROUP):
+    for base in range(0, count, group):
+        for k in range(max(base, 1), base + group):
             routed(k).wait_recv()
-        part = pl.ds(base, GROUP)
-        place = recv[part, 0].astype(jnp.int32) - 1
-        parts[0, part] = (place >> (width.bit_length() - 1)).astype(F32)
-        parts[1, part] = (place & (width - 1)).astype(F32)
-        parts[2, part], parts[3, part] = split(recv[part, 1])
-        parts[4, part], parts[5, part] = split(recv[part, 2])
+        cell, real, imag = [
+            jnp.concatenate(
+                [recv[k, kind][:, :capacity] for k in range(base, base + group)], axis=1
+            )
+            for kind in range(KINDS)
+        ]
+        cell = cell.astype(jnp.int32) - 1
+        line_of = cell >> (width.bit_length() - 1)
+        place = (cell & (width - 1)) + jnp.where(line_of >= half, width, 0)
+        at = base // group
+        parts[at, 0] = (line_of & (half - 1)).astype(F32)
+        parts[at, 1] = jnp.where(cell < 0, -1, place).astype(F32)
+        parts[at, 2], parts[at, 3] = split(real)
+        parts[at, 4], parts[at, 5] = split(imag)
         each_shot(functools.partial(gather, base))
 
     def apply_first(s):
@@ -378,13 +390,14 @@
     shots, block = rec_local.shape
     capacity = 3 * block // count
     slots = -(-capacity // LANES) * LANES
+    group = min(count, SPAN // capacity)
     vmem = pl.BlockSpec(memory_space=pltpu.VMEM)
     hbm = pl.BlockSpec(memory_space=pltpu.HBM)
     smem = pl.BlockSpec(memory_space=pltpu.SMEM)
     pair = pltpu.VMEM((shots, 2, cells, width), F32)
     dma = pltpu.SemaphoreType.DMA
     wavefield, updated = pl.pallas_call(
-        functools.partial(kernel, count, depth, height, slots),
+        functools.partial(kernel, count, depth, height, slots, capacity),
         out_shape=(
             jax.ShapeDtypeStruct((2, shots, cells, width), F32),
             jax.ShapeDtypeStruct((cells, width), F32),
@@ -398,12 +411,12 @@
             pltpu.VMEM((shots, 1, block), jnp.int32),
             pltpu.VMEM((shots, block), jnp.int32),
             pltpu.VMEM((2, shots, block), F32),
-            pltpu.VMEM((shots, cells, 5 * width), F32),
-            pltpu.VMEM((shots, 16, block), F32),
-            pltpu.VMEM((count * shots, block), F32),
+            pltpu.VMEM((shots, 5 * cells // 2, 2 * width), F32),
+            pltpu.VMEM((shots, 2 * KINDS, block), F32),
+            pltpu.VMEM((shots, block), F32),
             pltpu.VMEM((count, KINDS, shots, slots), F32),
             pltpu.VMEM((count, KINDS, shots, slots), F32),
-            pltpu.VMEM((6, count, shots, slots), F32),
+            pltpu.VMEM((count // group, 6, shots, group * capacity), F32),
             pltpu.VMEM((shots, cells, width), F32),
             pair, pair, pair, pair, pair,
             pltpu.VMEM((3, 2, shots, 2, height, width), F32),

time: 54 us -> 45.2 us (0.84)
  Pallas kernels: 50.1 us -> 41.3 us
    pallas_call x1, Pallas kernels: 50.1 us -> 41.3 us  [local(): pl.pallas_call(functools.partial(kernel, count, depth, height, slots, cap...]
where the time goes in v3:
time: 45.2 us; the launch traced here: 44.9 us
  Pallas kernels  41.3 us (91%)
  local copies, waits for them, and re-layouts  2.95 us (7%)
  between operations  0.65 us (1%)
    pallas_call x1, Pallas kernels, local(): pl.pallas_call(functools.partial(kernel, count, depth, height, slots, cap...  41.3 us
    unnamed x4, local copies, waits for them, and re-layouts  2.95 us

profile of v3, /device:TPU:0, one launch (start us, length us, event | category | flops | bytes accessed | tf_op | source)
XLA Modules:
  0.0 44.9 jit_solution(13474045016809721536)
XLA Ops:
  0.6 41.3 %shard_map.86 = (f32[2,8,128,128]{3,2,1,0:T(8,128)}, f32[128,128]{1,0:T(8,128)}) custom-call(f32[128,128]{1,0:T(8,128)} %bitcast.6, s32[128,128]{1,0:T(8,128)} %bitcast.7, s32[8]{0:T(128)} %cell_ref.1, f32[2,8]{1,0:T(2,128)} %amp_ref.1, s32[8,1,512]{2,1,0:T(1,128)} %bitcast.9, s32[8,512]{1,0:T(8,128)} %loc_in.1, f32[2,8,512]{2,1,0:T(8,128)} %dat_in.1), custom_call_target="tpu_custom_call" | custom-call | tf_op jit(solution)/shard_map/pallas_call | solution.py:399
  42.0 0.0 copy-start
  42.0 2.3 %copy.11 = f32[2,8,4,32,128]{4,3,2,1,0:T(8,128)} copy(f32[2,8,4,32,128]{4,3,2,1,0:T(8,128)} %bitcast.5) | data formatting | bytes 2097152
  44.3 0.0 copy-done
  44.3 0.6 %copy.12 = f32[4,32,128]{2,1,0:T(8,128)} copy(f32[4,32,128]{2,1,0:T(8,128)S(1)} %bitcast.8) | data formatting | bytes 131072
Async XLA Ops:
  42.0 2.3 %copy-start = (f32[128,128]{1,0:T(8,128)S(1)}, f32[128,128]{1,0:T(8,128)}, u32[]{:S(2)}) copy-start(f32[128,128]{1,0:T(8,128)} %get-tuple-element.5) | copy-start | bytes 196612

commit v4 on v3

--- a/solution.py
+++ b/solution.py
@@ -41,8 +41,8 @@
     wave_out, upd_ref,
     wave_ref, slow_ref, absorb_ref, own_ref, loc_ref, dat_ref, sums,
     feats, ranks, send, recv, parts, weight, field, image, normal, rest, rest_image,
-    halo, stat_a, note_a, all_a, stat_b, note_b, all_b, scal,
-    load_s, store_s, route_s, route_r, sum_s, sum_r, halo_s, halo_r,
+    shell, cover, cover_in, halo, stat_a, note_a, all_a, stat_b, note_b, all_b, scal,
+    load_s, store_s, route_s, route_r, sum_s, sum_r, halo_s, halo_r, cover_s, cover_r,
 ):
     me = lax.axis_index("slab")
     shots, block = loc_ref.shape
@@ -151,38 +151,54 @@
         return jnp.abs(z_of - plane) + jnp.abs(y_of - line) + jnp.abs(x_of - place)
 
     def laplace(centre, low, high):
-        beside = jnp.concatenate([centre[height:], high], axis=0)
-        beside = beside + jnp.concatenate([low, centre[:-height]], axis=0)
-        beside = beside + jnp.where(at_top, 0.0, pltpu.roll(centre, 1, 0))
-        beside = beside + jnp.where(at_bottom, 0.0, pltpu.roll(centre, cells - 1, 0))
-        beside = beside + jnp.where(at_left, 0.0, pltpu.roll(centre, 1, 1))
-        beside = beside + jnp.where(at_right, 0.0, pltpu.roll(centre, width - 1, 1))
+        rows = centre.shape[0]
+        beside = jnp.concatenate([centre[height:], high] if rows > height else [high], axis=0)
+        beside = beside + jnp.concatenate([low, centre[:-height]] if rows > height else [low], axis=0)
+        beside = beside + jnp.where(at_top[:rows], 0.0, pltpu.roll(centre, 1, 0))
+        beside = beside + jnp.where(at_bottom[:rows], 0.0, pltpu.roll(centre, rows - 1, 0))
+        beside = beside + jnp.where(at_left[:rows], 0.0, pltpu.roll(centre, 1, 1))
+        beside = beside + jnp.where(at_right[:rows], 0.0, pltpu.roll(centre, width - 1, 1))
         return 6.0 * centre - beside
 
-    def helmholtz(real, imag, low, high, sign):
-        out_r = laplace(real, low[0], high[0]) - coeff * real + sign * lossy * imag
-        out_i = laplace(imag, low[1], high[1]) - coeff * imag - sign * lossy * real
+    def helmholtz(real, imag, low, high, sign, cover=None):
+        size, loss = (coeff, lossy) if cover is None else cover
+        out_r = laplace(real, low[0], high[0]) - size * real + sign * loss * imag
+        out_i = laplace(imag, low[1], high[1]) - size * imag - sign * loss * real
         return out_r, out_i
 
-    for step in range(3):
-        @pl.when(me == 0)
-        def _(step=step):
-            halo[step, 0] = jnp.zeros(halo.shape[2:], F32)
-
-        @pl.when(me == count - 1)
-        def _(step=step):
-            halo[step, 1] = jnp.zeros(halo.shape[2:], F32)
+    for side, last in enumerate((0, count - 1)):
+        @pl.when(me == last)
+        def _(side=side):
+            shell[side] = jnp.zeros(shell.shape[1:], F32)
+            halo[1, side] = jnp.zeros(halo.shape[2:], F32)
+            cover_in[side] = jnp.zeros(cover_in.shape[1:], F32)
+
+    for side, at in enumerate((cells - height, 0)):
+        cover[side, 0] = coeff[at : at + height]
+        cover[side, 1] = lossy[at : at + height]
 
     def edge(step, ref, s, side):
         target = me + 1 if side == 0 else me - 1
-        at = cells - height if side == 0 else 0
+        deep = 2 * height if step == 0 else height
+        at = cells - deep if side == 0 else 0
+        landing = shell.at[side, s] if step == 0 else halo.at[step - 1, side, s]
         return pltpu.make_async_remote_copy(
-            src_ref=ref.at[s, :, pl.ds(at, height), :], dst_ref=halo.at[step, side, s],
+            src_ref=ref.at[s, :, pl.ds(at, deep), :], dst_ref=landing,
             send_sem=halo_s.at[step, side, s], recv_sem=halo_r.at[step, side, s],
             device_id={"slab": target}, device_id_type=MESH,
         )
 
     has = [me > 0, me < count - 1]
+
+    def cover_edge(side):
+        return pltpu.make_async_remote_copy(
+            src_ref=cover.at[side], dst_ref=cover_in.at[side],
+            send_sem=cover_s.at[side], recv_sem=cover_r.at[side],
+            device_id={"slab": me + 1 if side == 0 else me - 1}, device_id_type=MESH,
+        )
+
+    pl.when(has[1])(lambda: cover_edge(0).start())
+    pl.when(has[0])(lambda: cover_edge(1).start())
 
     def send_edges(step, ref, s):
         pl.when(has[1])(lambda: edge(step, ref, s, 0).start())
@@ -285,13 +301,30 @@
         parts[at, 4], parts[at, 5] = split(imag)
         each_shot(functools.partial(gather, base))
 
+    pl.when(has[0])(lambda: cover_edge(0).wait_recv())
+    pl.when(has[1])(lambda: cover_edge(1).wait_recv())
+
     def apply_first(s):
         wait_edges(0, field, s)
         r, i = field[s, 0], field[s, 1]
-        out_r, out_i = helmholtz(r, i, halo[0, 0, s], halo[0, 1, s], 1.0)
+        low, high = shell[0, s], shell[1, s]
+        out_r, out_i = helmholtz(r, i, low[:, height:], high[:, :height], 1.0)
         image[s, 0] = out_r
         image[s, 1] = out_i
-        send_edges(1, image, s)
+        before_r, before_i = helmholtz(
+            low[0, height:], low[1, height:], low[:, :height],
+            (r[:height], i[:height]), 1.0, (cover_in[0, 0], cover_in[0, 1]),
+        )
+        after_r, after_i = helmholtz(
+            high[0, :height], high[1, :height], (r[-height:], i[-height:]),
+            high[:, height:], 1.0, (cover_in[1, 0], cover_in[1, 1]),
+        )
+        inner_low = jnp.where(me > 0, 1.0, 0.0)
+        inner_high = jnp.where(me < count - 1, 1.0, 0.0)
+        halo[0, 0, s, 0] = inner_low * before_r
+        halo[0, 0, s, 1] = inner_low * before_i
+        halo[0, 1, s, 0] = inner_high * after_r
+        halo[0, 1, s, 1] = inner_high * after_i
         size = r * r + i * i
         stat_a[0, pl.ds(s, 1), :] = along(size)
         stat_a[1, pl.ds(s, 1), :] = along(out_r * out_r + out_i * out_i + weight[s] * size)
@@ -300,8 +333,7 @@
     share(0, stat_a, note_a, all_a)
 
     def apply_back(s):
-        wait_edges(1, image, s)
-        out_r, out_i = helmholtz(image[s, 0], image[s, 1], halo[1, 0, s], halo[1, 1, s], -1.0)
+        out_r, out_i = helmholtz(image[s, 0], image[s, 1], halo[0, 0, s], halo[0, 1, s], -1.0)
         normal[s, 0] = out_r + weight[s] * field[s, 0]
         normal[s, 1] = out_i + weight[s] * field[s, 1]
         send_edges(2, normal, s)
@@ -316,8 +348,8 @@
         step = scal[0, pl.ds(s, 1), :]
         r = field[s, 0] - step * normal[s, 0]
         i = field[s, 1] - step * normal[s, 1]
-        low = halo[0, 0, s] - step[None] * halo[2, 0, s]
-        high = halo[0, 1, s] - step[None] * halo[2, 1, s]
+        low = shell[0, s][:, height:] - step[None] * halo[1, 0, s]
+        high = shell[1, s][:, :height] - step[None] * halo[1, 1, s]
         out_r, out_i = helmholtz(r, i, low, high, 1.0)
         rest[s, 0] = r
         rest[s, 1] = i
@@ -369,10 +401,11 @@
 
     def drain(s):
         sent_edges(0, field, s)
-        sent_edges(1, image, s)
         sent_edges(2, normal, s)
         store(s).wait()
 
+    pl.when(has[1])(lambda: cover_edge(0).wait_send())
+    pl.when(has[0])(lambda: cover_edge(1).wait_send())
     each_shot(drain)
 
     def drain_small(k):
@@ -419,7 +452,10 @@
             pltpu.VMEM((count // group, 6, shots, group * capacity), F32),
             pltpu.VMEM((shots, cells, width), F32),
             pair, pair, pair, pair, pair,
-            pltpu.VMEM((3, 2, shots, 2, height, width), F32),
+            pltpu.VMEM((2, shots, 2, 2 * height, width), F32),
+            pltpu.VMEM((2, 2, height, width), F32),
+            pltpu.VMEM((2, 2, height, width), F32),
+            pltpu.VMEM((2, 2, shots, 2, height, width), F32),
             pltpu.VMEM((2, shots, LANES), F32),
             pltpu.VMEM((1, LANES), F32),
             pltpu.VMEM((count, 1, LANES), F32),
@@ -429,7 +465,7 @@
             pltpu.VMEM((3, shots, LANES), F32),
             dma((5,)), dma((shots,)), dma((count,)), dma((count,)),
             dma((2, count)), dma((2, count)),
-            dma((3, 2, shots)), dma((3, 2, shots)),
+            dma((3, 2, shots)), dma((3, 2, shots)), dma((2,)), dma((2,)),
         ],
         compiler_params=pltpu.CompilerParams(
             collective_id=0, has_side_effects=True, vmem_limit_bytes=60 * 1024 * 1024

time: 45.2 us -> 48.1 us (1.064)
  Pallas kernels: 41.3 us -> 44.3 us
    pallas_call x1, Pallas kernels: 41.3 us -> 44.3 us  [local(): pl.pallas_call(functools.partial(kernel, count, depth, height, slots, cap...]
where the time goes in v4:
time: 48.1 us; the launch traced here: 47.9 us
  Pallas kernels  44.3 us (92%)
  local copies, waits for them, and re-layouts  2.95 us (6%)
  between operations  0.65 us (1%)
    pallas_call x1, Pallas kernels, local(): pl.pallas_call(functools.partial(kernel, count, depth, height, slots, cap...  44.3 us
    unnamed x4, local copies, waits for them, and re-layouts  2.95 us

profile of v4, /device:TPU:0, one launch (start us, length us, event | category | flops | bytes accessed | tf_op | source)
XLA Modules:
  0.0 47.9 jit_solution(2725459615019302366)
XLA Ops:
  0.6 44.3 %shard_map.86 = (f32[2,8,128,128]{3,2,1,0:T(8,128)}, f32[128,128]{1,0:T(8,128)}) custom-call(f32[128,128]{1,0:T(8,128)} %bitcast.6, s32[128,128]{1,0:T(8,128)} %bitcast.7, s32[8]{0:T(128)} %cell_ref.1, f32[2,8]{1,0:T(2,128)} %amp_ref.1, s32[8,1,512]{2,1,0:T(1,128)} %bitcast.9, s32[8,512]{1,0:T(8,128)} %loc_in.1, f32[2,8,512]{2,1,0:T(8,128)} %dat_in.1), custom_call_target="tpu_custom_call" | custom-call | tf_op jit(solution)/shard_map/pallas_call | solution.py:432
  44.9 0.0 copy-start
  44.9 2.3 %copy.11 = f32[2,8,4,32,128]{4,3,2,1,0:T(8,128)} copy(f32[2,8,4,32,128]{4,3,2,1,0:T(8,128)} %bitcast.5) | data formatting | bytes 2097152
  47.3 0.0 copy-done
  47.3 0.6 %copy.12 = f32[4,32,128]{2,1,0:T(8,128)} copy(f32[4,32,128]{2,1,0:T(8,128)S(1)} %bitcast.8) | data formatting | bytes 131072
Async XLA Ops:
  44.9 2.3 %copy-start = (f32[128,128]{1,0:T(8,128)S(1)}, f32[128,128]{1,0:T(8,128)}, u32[]{:S(2)}) copy-start(f32[128,128]{1,0:T(8,128)} %get-tuple-element.5) | copy-start | bytes 196612
